TPU v7x, 512 devices: a whole 4x8x8 slice. The times are simulated.
512 devices in a mesh: dp: 16 (over y, core), expert: 32 (over z, x).
Axes of the slice: x: 4, y: 8, z: 8, core: 2. Of those that a mesh axis runs over, the one named last changes fastest.
Arguments:
- stream_q: bfloat16 [4096, 4096], P('dp', 'expert'), may hold values from -6 to 6
- stream_k: bfloat16 [4096, 4096], P('dp', 'expert'), may hold values from -6 to 6
- stream_v: bfloat16 [4096, 4096], P('dp', 'expert'), may hold values from -6 to 6
- conv_taps: float32 [3, 3, 4096], P(None, None, 'expert'), may hold values from -14 to 14
- norm_gain: bfloat16 [4096], P('expert'), may hold values from 0.3984375 to 1.59375
- slot_token: int32 [16, 384], P('dp'), may hold values from 0 to 256, as said below
- expert_count: int32 [16, 2], P('dp'), may hold values from 0 to 256, as said below
- route_prob: float32 [4096], P('dp'), may hold values from 0.25 to 1
- w_proj: bfloat16 [4096, 2, 8192], P('dp', None, 'expert'), may hold values from -0.09375 to 0.09375
- grad_out: bfloat16 [4096, 8192], P('dp', 'expert'), may hold values from -0.75 to 0.75
Outputs:
- activation: bfloat16 [4096, 8192], P('dp', 'expert')
- weight_grad: float32 [4096, 2, 8192], P('dp', None, 'expert')
Inputs may be any that keep to these rules, and one draw needn't show every extreme that they name: `slot_token`: for each index of dp the slots hold its 256 local token numbers, each exactly once, grouped by expert in expert order; each group starts at a multiple of 128 and is padded with the value 256 up to a multiple of 128; all slots after the last group hold 256. `expert_count`: the size of each expert's group in slot_token, before padding; each row sums to 256.
All inputs are finite; a program needn't handle non-finite values.
Results may differ from a plain program's by a relative error of at most 0.023.
Values may be sent and summed in bfloat16 or wider, within the bound.
No kernel may reach another device: no remote copies, remote signals or barrier semaphores. Data moves between devices by JAX's collectives and lax.ppermute only.
A program may use at most 64 MiB of HBM per device.

v0:
```python
import jax
import jax.numpy as jnp
from jax import lax
from jax.sharding import PartitionSpec as P

D = 4096
BLOCK = 128
epsilon = 1e-06


def from_behind(value, axis, steps):
    count = lax.axis_size(axis)
    leading, last = (max(0, -steps), min(count, count - steps))
    return lax.ppermute(value, axis, [(source, source + steps) for source in range(leading, last)])


def block_owner(counts, num_blocks):
    padded = (counts + BLOCK - 1) // BLOCK * BLOCK
    ends = jnp.cumsum(padded)
    starts = jnp.arange(num_blocks, dtype=jnp.int32) * BLOCK
    owner = jnp.sum((starts[:, None] >= ends[None, :]).astype(jnp.int32), axis=1)
    return jnp.minimum(owner, counts.shape[0] - 1)


def on_device(
    stream_q,
    stream_k,
    stream_v,
    conv_taps,
    norm_gain,
    slot_token,
    expert_count,
    route_prob,
    w_proj,
    grad_out,
):
    stacked = jnp.stack([stream_q, stream_k, stream_v])
    before = from_behind(stacked[:, -2:, :], "dp", 1)
    extended = jnp.concatenate([before, stacked], axis=1).astype(jnp.float32)
    convolved = (
        conv_taps[:, 0, None, :] * extended[:, 2:]
        + conv_taps[:, 1, None, :] * extended[:, 1:-1]
        + conv_taps[:, 2, None, :] * extended[:, :-2]
    )
    mixed = (convolved[0] * convolved[1] * convolved[2]).astype(jnp.bfloat16)
    mixed_f = mixed.astype(jnp.float32)
    total = lax.psum(jnp.sum(mixed_f * mixed_f, axis=1), "expert")
    inv_rms = lax.rsqrt(total / D + epsilon)
    normed = (mixed_f * inv_rms[:, None] * norm_gain.astype(jnp.float32)).astype(jnp.bfloat16)
    gathered = lax.all_gather(normed, "expert", axis=1, tiled=True)
    tok_count = gathered.shape[0]
    slots = slot_token[0]
    num_blocks = slots.shape[0] // BLOCK
    owner = block_owner(expert_count[0], num_blocks)
    padded_rows = jnp.concatenate(
        [gathered, jnp.zeros((1, gathered.shape[1]), jnp.bfloat16)], axis=0
    )
    x_blocks = padded_rows[slots].reshape(num_blocks, BLOCK, gathered.shape[1])
    hid_local = w_proj.shape[2]
    experts_here = w_proj.shape[1]
    selector = (owner[:, None] == jnp.arange(experts_here, dtype=jnp.int32)[None, :]).astype(
        jnp.bfloat16
    )
    columns = x_blocks
    chosen_w = jnp.einsum(
        "neh,be->bnh",
        lax.all_gather(w_proj, "dp", axis=0, tiled=True),
        selector,
        preferred_element_type=jnp.float32,
    ).astype(jnp.bfloat16)
    pre_act = jnp.einsum("brn,bnh->brh", columns, chosen_w, preferred_element_type=jnp.float32)
    pre_act = pre_act.reshape(num_blocks * BLOCK, hid_local)
    slot_prob = jnp.concatenate([route_prob, jnp.zeros((1,), jnp.float32)])[slots][:, None]
    sigmoid_z = jax.nn.sigmoid(pre_act)
    hidden = (slot_prob * pre_act * sigmoid_z).astype(jnp.bfloat16)
    activation = (
        jnp.zeros((tok_count + 1, hid_local), jnp.bfloat16).at[slots].set(hidden)[:tok_count]
    )
    slot_grad = jnp.concatenate([grad_out, jnp.zeros((1, hid_local), jnp.bfloat16)], axis=0)[
        slots
    ].astype(jnp.float32)
    grad_pre = (slot_grad * slot_prob * sigmoid_z * (1.0 + pre_act * (1.0 - sigmoid_z))).astype(
        jnp.bfloat16
    )
    grad_blocks = grad_pre.reshape(num_blocks, BLOCK, hid_local)
    masked_grad = grad_blocks[None, :, :, :] * selector.T[:, :, None, None]
    columns = x_blocks
    weight_grad = lax.psum_scatter(
        jnp.einsum(
            "brd,ebrh->deh", columns, masked_grad, preferred_element_type=jnp.float32
        ).astype(jnp.bfloat16),
        "dp",
        scatter_dimension=0,
        tiled=True,
    ).astype(jnp.float32)
    return (activation, weight_grad)


def solution(mesh):
    placed = (
        P("dp", "expert"),
        P("dp", "expert"),
        P("dp", "expert"),
        P(None, None, "expert"),
        P("expert"),
        P("dp", None),
        P("dp", None),
        P("dp"),
        P("dp", None, "expert"),
        P("dp", "expert"),
    )
    return jax.shard_map(
        on_device,
        mesh=mesh,
        in_specs=placed,
        out_specs=(P("dp", "expert"), P("dp", None, "expert")),
        check_vma=False,
    )
```

profile of v0, /device:TPU:29, one launch (start us, length us, event | category | flops | bytes accessed | tf_op | source)
XLA Modules:
  0.0 303.6 jit_solution(1994741817525698117)
XLA Ops:
  7.2 0.7 pad_maximum_fusion.1
  8.0 5.0 %collective-permute-start = (bf16[3,2,128]{2,1,0:T(2,128)(2,1)S(1)}, bf16[3,2,128]{2,1,0:T(2,128)(2,1)S(1)}, u32[]{:S(2)}, u32[]{:S(2)}) collective-permute-start(bf16[3,2,128]{2,1,0:T(2,128)(2,1)S(1)} %pad_maximum_fusion.1), channel_id=1, source_target_pairs={{0,32},{32,64},{64,96},{96,128},{128,160},{160,192},{192,224},{224... | collective-permute-start | bytes 4616 | tf_op jit(solution)/shard_map/ppermute | solution.py:14
  12.9 0.8 fusion.29
  13.8 0.7 convert_element_type.59
  14.4 0.9 maximum_convert_fusion
  15.6 62.6 %psum.7 = f32[256]{0:T(256)S(1)} all-reduce(f32[256]{0:T(256)S(1)} %get-tuple-element.10), channel_id=1, replica_groups=mesh['dp'=16,'expert'=32] {'expert'}, use_global_device_ids=true, to_apply=%region_1.0 | all-reduce | flops 256 | bytes 2048 | tf_op jit(solution)/shard_map/psum | solution.py:47
  78.2 0.7 fusion.17
  79.0 0.7 all-gather.5.cloned.1.call-update
  79.8 0.7 pad_maximum_fusion
  80.5 0.7 fusion.24
  81.2 2.8 gather_fusion
  84.0 2.6 gather_fusion.2
  86.6 0.2 reduce-window.8
  86.9 81.5 %all-gather.3.cloned.1.call-done = bf16[256,4096]{1,0:T(8,128)(2,1)} async-done(((bf16[256,128]{1,0:T(8,128)(2,1)}), bf16[256,4096]{1,0:T(8,128)(2,1)}) %all-gather.3.cloned.1.call-update) | async-done | bytes 2097168 | tf_op jit(solution)/shard_map/all_gather | solution.py:50
  168.4 1.8 concatenate.14
  170.1 4.1 %gather_fusion.1 = bf16[384,4096]{1,0:T(8,128)(2,1)} fusion(bf16[257,4096]{1,0:T(8,128)(2,1)S(1)} %concatenate.14, s32[1024]{0:T(1024)S(1)} %pad_clamp_fusion), kind=kCustom, calls=%fused_computation.1 | custom fusion | bytes 6292992 | tf_op jit(solution)/shard_map/gather | solution.py:58
  174.2 42.7 %all-gather.5.cloned.1.call-done = bf16[4096,2,256]{2,1,0:T(2,128)(2,1)} async-done(((bf16[256,2,256]{2,1,0:T(2,128)(2,1)}), bf16[4096,2,256]{2,1,0:T(2,128)(2,1)}) %all-gather.5.cloned.1.call-update) | async-done | bytes 4194320 | tf_op jit(solution)/shard_map/all_gather | solution.py:67
  217.0 7.5 %convolution_convert_fusion = bf16[3,4096,256]{2,0,1:T(4,128)(2,1)S(1)} fusion(bf16[4096,2,256]{2,1,0:T(2,128)(2,1)} %all-gather.5.cloned.1.call-done, s32[3]{0:T(128)S(1)} %broadcast_minimum_fusion), kind=kOutput, calls=%fused_computation.5 | convolution fusion | flops 15728646 | bytes 10485772 | tf_op jit(solution)/shard_map/neh,be->bnh/dot_general | solution.py:65
  224.5 1.3 fusion.6
  225.8 4.4 %bitcast_convert_fusion = bf16[4096,2,256]{2,0,1:T(8,128)(2,1)} fusion(bf16[3,128,4096,1]{2,1,0,3:T(8,128)(2,1)S(1)} %bitcast.50, bf16[2,3]{1,0:T(2,128)(2,1)S(1)} %compare_convert_fusion, bf16[3,128,256]{2,1,0:T(8,128)(2,1)S(1)} %get-tuple-element.15), kind=kOutput, calls=%fused_computation.4 | convolution fusion | flops 1613496320 | bytes 7536652 | tf_op jit(solution)/shard_map/brd,ebrh->deh/dot_general | solution.py:89
  230.3 1.9 scatter_custom_fusion
  232.2 0.7 slice.56
  232.8 62.2 %reduce-scatter.2.cloned.1.call-done = bf16[256,2,256]{2,0,1:T(8,128)(2,1)} async-done(((bf16[4096,2,256]{2,0,1:T(8,128)(2,1)}), bf16[256,2,256]{2,0,1:T(8,128)(2,1)}) %reduce-scatter.2.cloned.1.call-update) | async-done | bytes 262160 | tf_op jit(solution)/shard_map/reduce_scatter | solution.py:88
  295.1 2.0 copy.21
  (27 shorter events, 0.7 us)
Async XLA Ops:
  7.2 76.8 %copy-start.2 = (bf16[256,256]{1,0:T(8,128)(2,1)S(1)}, bf16[256,256]{1,0:T(8,128)(2,1)}, u32[]{:S(2)}) copy-start(bf16[256,256]{1,0:T(8,128)(2,1)} %param.19) | copy-start | bytes 393220
  7.2 79.4 %copy-start.3 = (s32[1,2]{1,0:T(1,128)S(1)}, s32[1,2]{1,0:T(1,128)}, u32[]{:S(2)}) copy-start(s32[1,2]{1,0:T(1,128)} %param.16) | copy-start | bytes 28
  7.2 161.2 %all-gather.3.cloned.1.call-start = ((), (), s32[]{:S(2)}) async-start(), calls=%async_computation.1 | async-start | bytes 2162688 | tf_op jit(solution)/shard_map/all_gather | solution.py:50
  8.0 6.5 %collective-permute-start = (bf16[3,2,128]{2,1,0:T(2,128)(2,1)S(1)}, bf16[3,2,128]{2,1,0:T(2,128)(2,1)S(1)}, u32[]{:S(2)}, u32[]{:S(2)}) collective-permute-start(bf16[3,2,128]{2,1,0:T(2,128)(2,1)S(1)} %pad_maximum_fusion.1), channel_id=1, source_target_pairs={{0,32},{32,64},{64,96},{96,128},{128,160},{160,192},{192,224},{224... | collective-permute-start | bytes 4616 | tf_op jit(solution)/shard_map/ppermute | solution.py:14
  79.0 138.0 %all-gather.5.cloned.1.call-start = ((), (), s32[]{:S(2)}) async-start(), calls=%async_computation.2 | async-start | bytes 4456448 | tf_op jit(solution)/shard_map/all_gather | solution.py:67
  79.7 215.3 %reduce-scatter.2.cloned.1.call-start = ((), (), s32[]{:S(2)}) async-start(), calls=%async_computation.3 | async-start | bytes 4456448 | tf_op jit(solution)/shard_map/reduce_scatter | solution.py:88
  174.2 50.2 %copy-start = (bf16[384,4096]{1,0:T(8,128)(2,1)S(1)}, bf16[384,4096]{1,0:T(8,128)(2,1)}, u32[]{:S(2)}) copy-start(bf16[384,4096]{1,0:T(8,128)(2,1)} %gather_fusion.1) | copy-start | bytes 9437188
  217.0 7.5 %copy-start.1 = (bf16[384,256]{1,0:T(8,128)(2,1)S(1)}, bf16[384,256]{1,0:T(8,128)(2,1)}, u32[]{:S(2)}) copy-start(bf16[384,256]{1,0:T(8,128)(2,1)} %gather_fusion.2) | copy-start | bytes 589828
Sparse Core Ops, SparseCore 0:
  79.1 89.2 all-gather.2
  170.5 46.4 all-gather.4
  230.3 64.7 reduce-scatter.1
where the time goes:
time: 304 us
  waiting for transfers between devices  187 us (62%)
  blocking collectives  62.6 us (21%)
  local copies, waits for them, and re-layouts  16.6 us (5%)
  between operations  13.9 us (5%)
  matrix products  13.1 us (4%)
  other arithmetic  5.15 us (2%)
  starting transfers between devices  5.08 us (2%)
    all_gather x1, waiting for transfers between devices, on_device(): gathered = lax.all_gather(normed, 'expert', axis=1, tiled=True)  81.5 us
    psum x1, blocking collectives, on_device(): total = lax.psum(jnp.sum(mixed_f * mixed_f, axis=1), 'expert')  62.6 us
    reduce_scatter x1, waiting for transfers between devices, on_device(): lax.psum_scatter(jnp.einsum('brd,ebrh->deh', columns, masked_grad, prefer...  62.2 us
    all_gather x1, waiting for transfers between devices, on_device(): lax.all_gather(w_proj, 'dp', axis=0, tiled=True)  42.7 us
    dot_general x1, matrix products, on_device(): jnp.einsum('neh,be->bnh', lax.all_gather(w_proj, 'dp', axis=0, tiled=True...  7.48 us
  transfers between devices with their start and end apart: 4, of which 3 were waited for; matrix products, arithmetic and copies ran while one was open for 6% of the time, Pallas kernels for 0%

commit v1 on v0

--- a/solution.py
+++ b/solution.py
@@ -44,7 +44,7 @@
     )
     mixed = (convolved[0] * convolved[1] * convolved[2]).astype(jnp.bfloat16)
     mixed_f = mixed.astype(jnp.float32)
-    total = lax.psum(jnp.sum(mixed_f * mixed_f, axis=1), "expert")
+    total = jnp.sum(lax.all_gather(jnp.sum(mixed_f * mixed_f, axis=1), "expert"), axis=0)
     inv_rms = lax.rsqrt(total / D + epsilon)
     normed = (mixed_f * inv_rms[:, None] * norm_gain.astype(jnp.float32)).astype(jnp.bfloat16)
     gathered = lax.all_gather(normed, "expert", axis=1, tiled=True)

time: 304 us -> 275 us (0.905)
  the two profiles are of different devices: /device:TPU:29 before, /device:TPU:25 now
where the time goes in v1:
time: 275 us
  waiting for transfers between devices  182 us (66%)
  blocking collectives  38.9 us (14%)
  local copies, waits for them, and re-layouts  16.6 us (6%)
  between operations  13.9 us (5%)
  matrix products  13.1 us (5%)
  other arithmetic  5.2 us (2%)
  starting transfers between devices  5.08 us (2%)
    all_gather x1, waiting for transfers between devices, on_device(): gathered = lax.all_gather(normed, 'expert', axis=1, tiled=True)  75.9 us
    reduce_scatter x1, waiting for transfers between devices, on_device(): lax.psum_scatter(jnp.einsum('brd,ebrh->deh', columns, masked_grad, prefer...  62.2 us
    all_gather x1, waiting for transfers between devices, on_device(): lax.all_gather(w_proj, 'dp', axis=0, tiled=True)  42.8 us
    all_gather x1, blocking collectives, on_device(): lax.all_gather(jnp.sum(mixed_f * mixed_f, axis=1), 'expert')  38.9 us
    dot_general x1, matrix products, on_device(): jnp.einsum('neh,be->bnh', lax.all_gather(w_proj, 'dp', axis=0, tiled=True...  7.48 us
  transfers between devices with their start and end apart: 4, of which 3 were waited for; matrix products, arithmetic and copies ran while one was open for 6% of the time, Pallas kernels for 0%

profile of v1, /device:TPU:25, one launch (start us, length us, event | category | flops | bytes accessed | tf_op | source)
XLA Modules:
  0.0 274.6 jit_solution(12499326009660245737)
XLA Ops:
  7.2 0.7 pad_maximum_fusion.1
  8.0 5.0 %collective-permute-start = (bf16[3,2,128]{2,1,0:T(2,128)(2,1)S(1)}, bf16[3,2,128]{2,1,0:T(2,128)(2,1)S(1)}, u32[]{:S(2)}, u32[]{:S(2)}) collective-permute-start(bf16[3,2,128]{2,1,0:T(2,128)(2,1)S(1)} %pad_maximum_fusion.1), channel_id=1, source_target_pairs={{0,32},{32,64},{64,96},{96,128},{128,160},{160,192},{192,224},{224... | collective-permute-start | bytes 4616 | tf_op jit(solution)/shard_map/ppermute | solution.py:14
  12.9 0.8 fusion.29
  13.8 0.7 convert_element_type.59
  14.4 0.9 maximum_convert_fusion
  15.6 38.9 %all-gather.1 = f32[32,1,256]{2,1,0:T(1,128)S(1)} all-gather(f32[1,1,256]{2,1,0:T(1,128)S(1)} %bitcast.61), channel_id=2, replica_groups=mesh['dp'=16,'expert'=32] {'expert'}, dimensions={0}, use_global_device_ids=true | all-gather | bytes 33792 | tf_op jit(solution)/shard_map/all_gather | solution.py:47
  54.6 0.7 fusion.17
  55.4 0.7 all-gather.7.cloned.1.call-update
  56.2 0.7 pad_maximum_fusion
  56.9 0.7 fusion.24
  57.6 2.8 %gather_fusion = f32[384]{0:T(512)S(1)} fusion(f32[257]{0:T(512)S(1)} %pad_maximum_fusion, s32[1024]{0:T(1024)S(1)} %pad_clamp_fusion), kind=kCustom, calls=%fused_computation | custom fusion | bytes 4608 | tf_op jit(solution)/shard_map/gather | solution.py:73
  60.4 2.6 gather_fusion.2
  63.0 0.2 reduce-window.8
  63.3 75.9 %all-gather.5.cloned.1.call-done = bf16[256,4096]{1,0:T(8,128)(2,1)} async-done(((bf16[256,128]{1,0:T(8,128)(2,1)}), bf16[256,4096]{1,0:T(8,128)(2,1)}) %all-gather.5.cloned.1.call-update) | async-done | bytes 2097168 | tf_op jit(solution)/shard_map/all_gather | solution.py:50
  139.2 1.8 concatenate.14
  141.0 4.1 %gather_fusion.1 = bf16[384,4096]{1,0:T(8,128)(2,1)} fusion(bf16[257,4096]{1,0:T(8,128)(2,1)S(1)} %concatenate.14, s32[1024]{0:T(1024)S(1)} %pad_clamp_fusion), kind=kCustom, calls=%fused_computation.1 | custom fusion | bytes 6292992 | tf_op jit(solution)/shard_map/gather | solution.py:58
  145.1 42.8 %all-gather.7.cloned.1.call-done = bf16[4096,2,256]{2,1,0:T(2,128)(2,1)} async-done(((bf16[256,2,256]{2,1,0:T(2,128)(2,1)}), bf16[4096,2,256]{2,1,0:T(2,128)(2,1)}) %all-gather.7.cloned.1.call-update) | async-done | bytes 4194320 | tf_op jit(solution)/shard_map/all_gather | solution.py:67
  187.9 7.5 %convolution_convert_fusion = bf16[3,4096,256]{2,0,1:T(4,128)(2,1)S(1)} fusion(bf16[4096,2,256]{2,1,0:T(2,128)(2,1)} %all-gather.7.cloned.1.call-done, s32[3]{0:T(128)S(1)} %broadcast_minimum_fusion), kind=kOutput, calls=%fused_computation.5 | convolution fusion | flops 15728646 | bytes 10485772 | tf_op jit(solution)/shard_map/neh,be->bnh/dot_general | solution.py:65
  195.4 1.3 fusion.6
  196.7 4.4 %bitcast_convert_fusion = bf16[4096,2,256]{2,0,1:T(8,128)(2,1)} fusion(bf16[3,128,4096,1]{2,1,0,3:T(8,128)(2,1)S(1)} %bitcast.51, bf16[2,3]{1,0:T(2,128)(2,1)S(1)} %compare_convert_fusion, bf16[3,128,256]{2,1,0:T(8,128)(2,1)S(1)} %get-tuple-element.15), kind=kOutput, calls=%fused_computation.4 | convolution fusion | flops 1613496320 | bytes 7536652 | tf_op jit(solution)/shard_map/brd,ebrh->deh/dot_general | solution.py:89
  201.3 1.9 scatter_custom_fusion
  203.1 0.7 slice.56
  203.8 62.2 %reduce-scatter.2.cloned.1.call-done = bf16[256,2,256]{2,0,1:T(8,128)(2,1)} async-done(((bf16[4096,2,256]{2,0,1:T(8,128)(2,1)}), bf16[256,2,256]{2,0,1:T(8,128)(2,1)}) %reduce-scatter.2.cloned.1.call-update) | async-done | bytes 262160 | tf_op jit(solution)/shard_map/reduce_scatter | solution.py:88
  266.0 2.0 copy.21
  (28 shorter events, 0.7 us)
Async XLA Ops:
  7.2 53.2 %copy-start.2 = (bf16[256,256]{1,0:T(8,128)(2,1)S(1)}, bf16[256,256]{1,0:T(8,128)(2,1)}, u32[]{:S(2)}) copy-start(bf16[256,256]{1,0:T(8,128)(2,1)} %param.19) | copy-start | bytes 393220
  7.2 55.8 %copy-start.3 = (s32[1,2]{1,0:T(1,128)S(1)}, s32[1,2]{1,0:T(1,128)}, u32[]{:S(2)}) copy-start(s32[1,2]{1,0:T(1,128)} %param.16) | copy-start | bytes 28
  7.2 132.0 %all-gather.5.cloned.1.call-start = ((), (), s32[]{:S(2)}) async-start(), calls=%async_computation.1 | async-start | bytes 2162688 | tf_op jit(solution)/shard_map/all_gather | solution.py:50
  8.0 6.5 %collective-permute-start = (bf16[3,2,128]{2,1,0:T(2,128)(2,1)S(1)}, bf16[3,2,128]{2,1,0:T(2,128)(2,1)S(1)}, u32[]{:S(2)}, u32[]{:S(2)}) collective-permute-start(bf16[3,2,128]{2,1,0:T(2,128)(2,1)S(1)} %pad_maximum_fusion.1), channel_id=1, source_target_pairs={{0,32},{32,64},{64,96},{96,128},{128,160},{160,192},{192,224},{224... | collective-permute-start | bytes 4616 | tf_op jit(solution)/shard_map/ppermute | solution.py:14
  55.4 132.5 %all-gather.7.cloned.1.call-start = ((), (), s32[]{:S(2)}) async-start(), calls=%async_computation.2 | async-start | bytes 4456448 | tf_op jit(solution)/shard_map/all_gather | solution.py:67
  56.1 209.9 %reduce-scatter.2.cloned.1.call-start = ((), (), s32[]{:S(2)}) async-start(), calls=%async_computation.3 | async-start | bytes 4456448 | tf_op jit(solution)/shard_map/reduce_scatter | solution.py:88
  145.1 50.3 %copy-start = (bf16[384,4096]{1,0:T(8,128)(2,1)S(1)}, bf16[384,4096]{1,0:T(8,128)(2,1)}, u32[]{:S(2)}) copy-start(bf16[384,4096]{1,0:T(8,128)(2,1)} %gather_fusion.1) | copy-start | bytes 9437188
  187.9 7.5 %copy-start.1 = (bf16[384,256]{1,0:T(8,128)(2,1)S(1)}, bf16[384,256]{1,0:T(8,128)(2,1)}, u32[]{:S(2)}) copy-start(bf16[384,256]{1,0:T(8,128)(2,1)} %gather_fusion.2) | copy-start | bytes 589828
Sparse Core Ops, SparseCore 0:
  55.5 83.6 all-gather.4
  141.3 46.5 all-gather.6
  201.2 64.7 reduce-scatter.1
